TPU v7x, 32 devices: a whole 2x2x4 slice. The times are simulated.
32 devices in a mesh: wide: 8 (over z, y), sub: 4 (over x, core).
Axes of the slice: x: 2, y: 2, z: 4, core: 2. Of those that a mesh axis runs over, the one named last changes fastest.
Arguments:
- lengths: int32 [4, 1024], P('sub', 'wide'), may hold values from 0 to 2048, as said below
- postings: bfloat16 [4, 16384, 128], P('sub', 'wide'), may hold values from -6 to 6
- codes: int32 [4, 8, 16384], P('sub', None, 'wide'), may hold values from 0 to 255
- rotation: bfloat16 [128, 128], replicated, may hold values from -0.5 to 0.5
Outputs:
- rotated_slices: bfloat16 [4, 128, 8192], P(None, 'sub', 'wide')
- codebook: float32 [8, 16, 256], P('sub')
Inputs may be any that keep to these rules, and one draw needn't show every extreme that they name: Each slab's lengths add up to 8192; no device holds more than 2048 rows in all; in each slab some device holds exactly 2048 rows, all in one list; lengths and whole devices may be empty.
All inputs are finite; a program needn't handle non-finite values.
Results may differ from a plain program's by a relative error of at most 0.0029.
Values may be sent and summed in bfloat16 or wider, within the bound.
A program may use at most 128 MiB of HBM per device.

v0:
```python
import jax
import jax.numpy as jnp
from jax import lax
from jax.sharding import PartitionSpec as P

KCODES = 256
SUBDIM = 16


def entering(part, axis, combine, identity):
    place = lax.axis_index(axis)
    gathered = lax.all_gather(part, axis)
    state = jnp.zeros_like(part) + jnp.asarray(identity, part.dtype)

    def one(turn, state):
        return combine(state, lax.dynamic_index_in_dim(gathered, turn, 0, False))

    return lax.fori_loop(0, place, one, state)


def add_counts(earlier, later):
    return earlier + later


def body(lengths, postings, codes, rotation):
    here = lax.axis_index("wide")
    capacity = postings.shape[1]
    per_shard = capacity // 2
    total = jnp.sum(lengths)
    offset = entering(total, "wide", add_counts, jnp.int32(0))
    marks = jnp.stack([offset, total]).astype(jnp.int32).reshape(1, 1, 2)
    code_rows = jnp.swapaxes(codes, 1, 2)
    targets = here * per_shard + jnp.arange(per_shard, dtype=jnp.int32)

    def place(carry, pieces, start):
        rows_piece, code_piece, mark_piece = pieces
        shards = mark_piece.shape[1]
        slots = rows_piece.shape[1] // shards

        def one_shard(shard, state):
            rows_acc, code_acc = state
            block_rows = lax.dynamic_slice_in_dim(rows_piece[0], shard * slots, slots, 0)
            block_codes = lax.dynamic_slice_in_dim(code_piece[0], shard * slots, slots, 0)
            source_start = mark_piece[0, shard, 0]
            source_total = mark_piece[0, shard, 1]
            within = targets - source_start
            usable = (within >= 0) & (within < source_total)
            safe = jnp.clip(within, 0, slots - 1)
            rows_acc = jnp.where(usable[:, None], jnp.take(block_rows, safe, axis=0), rows_acc)
            code_acc = jnp.where(usable[:, None], jnp.take(block_codes, safe, axis=0), code_acc)
            return (rows_acc, code_acc)

        return lax.fori_loop(0, shards, one_shard, carry)

    start_rows = jnp.zeros((per_shard, postings.shape[2]), jnp.bfloat16)
    start_codes = jnp.zeros((per_shard, codes.shape[1]), jnp.int32)
    kept, kept_code_rows = place(
        (start_rows, start_codes),
        (
            lax.all_gather(postings, "wide", axis=1, tiled=True),
            lax.all_gather(code_rows, "wide", axis=1, tiled=True),
            lax.all_gather(marks, "wide", axis=1, tiled=True),
        ),
        jnp.int32(0),
    )
    kept_codes = kept_code_rows.T
    rotated = jnp.einsum("rd,de->er", kept, rotation, preferred_element_type=jnp.float32).astype(
        jnp.bfloat16
    )
    slices, slice_codes = (
        lax.all_to_all(rotated[None], "sub", split_axis=1, concat_axis=0, tiled=True),
        lax.all_to_all(kept_codes[None], "sub", split_axis=1, concat_axis=0, tiled=True),
    )
    local_count = slice_codes.shape[1]
    centroid_ids = jnp.arange(KCODES, dtype=jnp.int32)
    sum_list = []
    count_list = []
    for local in range(local_count):
        values = slices[:, local * SUBDIM : (local + 1) * SUBDIM, :]
        onehot = (slice_codes[:, local, :, None] == centroid_ids).astype(jnp.bfloat16)
        sum_list.append(
            jnp.einsum("gde,gek->dk", values, onehot, preferred_element_type=jnp.float32)
        )
        count_list.append(jnp.sum(onehot.astype(jnp.float32), axis=(0, 1)))
    partial_sums = jnp.stack(sum_list)
    partial_counts = jnp.stack(count_list)
    full_sums, full_counts = lax.psum((partial_sums, partial_counts), "wide")
    codebook = full_sums / (full_counts[:, None, :] + 1.0)
    return (slices, codebook)


def solution(mesh):
    return jax.shard_map(
        body,
        mesh=mesh,
        in_specs=(P("sub", "wide"), P("sub", "wide", None), P("sub", None, "wide"), P()),
        out_specs=(P(None, "sub", "wide"), P("sub", None, None)),
        check_vma=False,
    )
```

profile of v0, /device:TPU:0, one launch (start us, length us, event | category | flops | bytes accessed | tf_op | source)
XLA Modules:
  0.0 384.8 jit_solution(17787069196864160257)
XLA Ops:
  7.2 0.7 all-gather.3.cloned.1.call-update
  7.9 1.2 dynamic-slice.6
  9.2 1.3 reduce_sum.27
  10.5 1.4 dynamic-update-slice
  11.9 13.2 %all-reduce = s32[8]{0:T(128)S(1)} all-reduce(s32[8]{0:T(128)S(1)} %dynamic-update-slice), channel_id=1, replica_groups=mesh['wide'=8,'sub'=4] {'wide'}, use_global_device_ids=true, to_apply=%add | all-reduce | flops 8 | bytes 64
  25.7 0.8 add_dynamic-update-slice_fusion
  26.5 15.9 %all-reduce.1 = s32[16]{0:T(128)S(1)} all-reduce(s32[16]{0:T(128)S(1)} %add_dynamic-update-slice_fusion), channel_id=2, replica_groups=mesh['wide'=8,'sub'=4] {'wide'}, use_global_device_ids=true, to_apply=%add.1 | all-reduce | flops 16 | bytes 128
  42.6 1.2 copy.17
  43.8 179.0 %all_gather.19 = s32[1,16384,8]{2,1,0:T(8,128)} all-gather(s32[1,2048,8]{2,1,0:T(8,128)S(1)} %bitcast.50), channel_id=1, replica_groups=mesh['wide'=8,'sub'=4] {'wide'}, dimensions={1}, use_global_device_ids=true | all-gather | bytes 589824 | tf_op jit(solution)/shard_map/all_gather | solution.py:61
  222.8 96.4 %while.27 = (s32[]{:T(128)}, bf16[1024,128]{1,0:T(8,128)(2,1)S(1)}, s32[1024,8]{1,0:T(8,128)S(1)}, s32[1,8,2]{1,2,0:T(2,128)S(1)}, bf16[1,16384,128]{2,1,0:T(8,1...) while((s32[]{:T(128)}, bf16[1024,128]{1,0:T(8,128)(2,1)S(1)}, ...), condition=%wide.region_4.5_spmd.clone, body=%wide.region_3.4_spmd.clone.sunk | while | flops 437255 | bytes 2689238 | solution.py:53
  222.8 1.3 dynamic-slice_bitcast_fusion.5
  224.7 0.7 fusion.22
  225.4 2.8 gather_fusion.1
  228.3 1.3 fusion.23
  230.0 1.1 dynamic-slice_bitcast_fusion.4
  231.1 3.2 gather_fusion
  234.8 1.3 dynamic-slice_bitcast_fusion.5
  236.8 0.7 fusion.22
  237.5 2.8 gather_fusion.1
  240.3 1.3 fusion.23
  242.1 1.1 dynamic-slice_bitcast_fusion.4
  243.2 3.2 gather_fusion
  246.9 1.3 dynamic-slice_bitcast_fusion.5
  248.8 0.7 fusion.22
  249.5 2.8 gather_fusion.1
  252.4 1.3 fusion.23
  254.1 1.1 dynamic-slice_bitcast_fusion.4
  255.2 3.2 gather_fusion
  258.9 1.3 dynamic-slice_bitcast_fusion.5
  261.6 2.8 gather_fusion.1
  264.4 1.3 fusion.23
  266.2 1.1 dynamic-slice_bitcast_fusion.4
  267.3 3.2 gather_fusion
  271.0 1.3 dynamic-slice_bitcast_fusion.5
  273.6 2.8 gather_fusion.1
  276.5 1.3 fusion.23
  278.2 1.1 dynamic-slice_bitcast_fusion.4
  279.3 3.2 gather_fusion
  283.0 1.3 dynamic-slice_bitcast_fusion.5
  285.0 0.7 fusion.22
  285.7 2.8 gather_fusion.1
  288.5 1.3 fusion.23
  290.3 1.1 dynamic-slice_bitcast_fusion.4
  291.4 3.2 gather_fusion
  295.1 1.3 dynamic-slice_bitcast_fusion.5
  297.7 2.8 gather_fusion.1
  300.6 1.3 fusion.23
  302.3 1.1 dynamic-slice_bitcast_fusion.4
  303.4 3.2 gather_fusion
  307.1 1.3 dynamic-slice_bitcast_fusion.5
  309.8 2.8 gather_fusion.1
  312.6 1.3 fusion.23
  314.4 1.1 dynamic-slice_bitcast_fusion.4
  315.5 3.2 gather_fusion
  320.0 3.3 all-to-all-start.1
  324.5 2.1 reduce.1
  326.6 0.9 reshape.97
  327.5 3.4 all-to-all-start
  331.1 0.8 convert_reduce_fusion.1
  331.9 0.8 convert_reduce_fusion
  332.7 4.2 %all-to-all-done = bf16[4,2,16384]{2,1,0:T(2,128)(2,1)S(1)} async-done(((bf16[4,2,16384]{2,1,0:T(2,128)(2,1)}), bf16[4,2,16384]{2,1,0:T(2,128)(2,1)S(1)}, u32[]{:S(2)}, u32[]{:S(2)}) %all-to-all-start) | async-done | bytes 262176 | tf_op jit(solution)/shard_map/all_to_all | solution.py:71
  337.3 1.4 fusion.13
  338.7 1.4 fusion.14
  340.1 37.2 %all-reduce.2 = (f32[2,16,256]{2,1,0:T(8,128)S(1)}, f32[2,256]{1,0:T(2,128)S(1)}) all-reduce(f32[2,16,256]{2,1,0:T(8,128)S(1)} %pad_maximum_fusion, f32[2,256]{1,0:T(2,128)S(1)} %pad_maximum_fusion.1), channel_id=1, replica_groups=mesh['wide'=8,'sub'=4] {'wide'}, use_global_device_ids=true, to_apply=%region_5.6 | all-reduce | flops 8704 | bytes 69632 | tf_op jit(solution)/shard_map/psum | solution.py:87
  (73 shorter events, 19.0 us)
Async XLA Ops:
  7.2 316.1 %copy-start = (bf16[128,128]{1,0:T(8,128)(2,1)S(1)}, bf16[128,128]{1,0:T(8,128)(2,1)}, u32[]{:S(2)}) copy-start(bf16[128,128]{1,0:T(8,128)(2,1)} %param.11) | copy-start | bytes 98308
  7.2 215.6 %all-gather.3.cloned.1.call-start = ((), (), s32[]{:S(2)}) async-start(), calls=%async_computation.2 | async-start | bytes 4718592 | tf_op jit(solution)/shard_map/all_gather | solution.py:60
  320.0 7.6 %all-to-all-start.1 = ((s32[1,8,1024]{2,0,1:T(1,128)}), s32[1,8,1024]{2,0,1:T(1,128)S(1)}, u32[]{:S(2)}, u32[]{:S(2)}) async-start(s32[1,8,1024]{2,0,1:T(1,128)} %broadcast_in_dim.90), calls=%async_computation.1 | async-start | bytes 65536 | tf_op jit(solution)/shard_map/all_to_all | solution.py:72
  327.5 9.4 %all-to-all-start = ((bf16[4,2,16384]{2,1,0:T(2,128)(2,1)}), bf16[4,2,16384]{2,1,0:T(2,128)(2,1)S(1)}, u32[]{:S(2)}, u32[]{:S(2)}) async-start(bf16[4,2,16384]{2,1,0:T(2,128)(2,1)} %reshape.97), calls=%async_computation | async-start | bytes 524288 | tf_op jit(solution)/shard_map/all_to_all | solution.py:71
  337.3 40.6 %copy-start.1 = (bf16[1,128,1024]{2,1,0:T(8,128)(2,1)}, bf16[1,128,1024]{2,1,0:T(8,128)(2,1)S(1)}, u32[]{:S(2)}) copy-start(bf16[1,128,1024]{2,1,0:T(8,128)(2,1)S(1)} %copy.21) | copy-start | bytes 786436
Sparse Core Ops, SparseCore 0:
  10.1 137.8 all-gather.2
where the time goes:
time: 386 us; the launch traced here: 385 us
  blocking collectives  245 us (63%)
  local copies, waits for them, and re-layouts  79.5 us (21%)
  other arithmetic  30 us (8%)
  between operations  14.8 us (4%)
  starting transfers between devices  6.71 us (2%)
  waiting for transfers between devices  4.89 us (1%)
    all_gather x1, blocking collectives, body(): lax.all_gather(code_rows, 'wide', axis=1, tiled=True)  179 us
    psum x1, blocking collectives, body(): full_sums, full_counts = lax.psum((partial_sums, partial_counts), 'wide')  37.2 us
    unnamed x2, blocking collectives  29.1 us
    gather x8, local copies, waits for them, and re-layouts, one_shard(): jnp.take(block_rows, safe, axis=0)  25.6 us
    gather x8, local copies, waits for them, and re-layouts, one_shard(): jnp.take(block_codes, safe, axis=0)  22.5 us
    dynamic_slice x8, local copies, waits for them, and re-layouts, one_shard(): lax.dynamic_slice_in_dim(code_piece[0], shard * slots, slots, 0)  10.4 us
    and x8, other arithmetic, one_shard(): usable = (within >= 0) & (within < source_total)  10.3 us
    dynamic_slice x8, local copies, waits for them, and re-layouts, one_shard(): lax.dynamic_slice_in_dim(rows_piece[0], shard * slots, slots, 0)  8.67 us
  transfers between devices with their start and end apart: 3, of which 1 were waited for; matrix products, arithmetic and copies ran while one was open for 3% of the time, Pallas kernels for 0%

commit v1 on v0

v1 whole, which is shorter than its diff:
```python
import functools

import jax
import jax.numpy as jnp
from jax import lax
from jax.experimental import pallas as pl
from jax.experimental.pallas import tpu as pltpu
from jax.sharding import PartitionSpec as P

KCODES = 256
SUBDIM = 16
LANES = 128
CODE_ROWS = 16
MESH = pl.DeviceIdType.MESH
NT = (((1,), (1,)), ((), ()))


def when(condition):
    if condition is True:
        return lambda body: body()
    return pl.when(condition)


def kernel(
    n_wide,
    n_sub,
    len_ref,
    post_ref,
    code_ref,
    rot_ref,
    out_ref,
    book_ref,
    lens,
    local,
    halves,
    arrived,
    final,
    slices,
    acc,
    parts,
    parts_in,
    tile,
    tiles_in,
    len_send,
    len_recv,
    wide_send,
    wide_recv,
    sub_send,
    sub_recv,
    part_send,
    part_recv,
    tile_send,
    tile_recv,
):
    me = lax.axis_index("wide")
    sub = lax.axis_index("sub")
    stages = n_wide.bit_length() - 1
    capacity, dims = post_ref.shape[1], post_ref.shape[2]
    spaces = code_ref.shape[1]
    shard = capacity // 2
    chunks, height, width = halves.shape[2:]
    own_dims = dims // n_sub
    own_spaces = spaces // n_sub
    n_tiles = parts.shape[0]
    columns = KCODES // LANES

    def wide_peer(distance):
        return lax.rem(me + distance, n_wide)

    def sub_peer(distance):
        return lax.rem(sub + distance, n_sub)

    barrier = pltpu.get_barrier_semaphore()
    for d in range(1, n_wide):
        pl.semaphore_signal(barrier, inc=1, device_id=(wide_peer(d), sub), device_id_type=MESH)
    for d in range(1, n_sub):
        pl.semaphore_signal(barrier, inc=1, device_id=(me, sub_peer(d)), device_id_type=MESH)
    pl.semaphore_wait(barrier, n_wide + n_sub - 2)

    len_copies = []
    for d in range(1, n_wide):
        copy = pltpu.make_async_remote_copy(
            src_ref=len_ref,
            dst_ref=lens.at[me],
            send_sem=len_send.at[d],
            recv_sem=len_recv.at[d],
            device_id=(wide_peer(d), sub),
            device_id_type=MESH,
        )
        copy.start()
        len_copies.append(copy)
    lens[me] = len_ref[...]

    turned = rot_ref[...].astype(jnp.float32).T.astype(jnp.bfloat16)
    blocks = capacity // LANES
    step = capacity // 4
    for i in range(4):
        span = slice(i * step, (i + 1) * step)
        block = lax.dot_general(turned, post_ref[0, span, :], NT, preferred_element_type=jnp.float32)
        block = block.astype(jnp.bfloat16)
        for k in range(step // LANES):
            local[i * (step // LANES) + k, :dims] = block[:, k * LANES : (k + 1) * LANES]
    spare = jnp.zeros((height - dims - spaces, LANES), jnp.float32)
    for k in range(blocks):
        labels = code_ref[0, :, k * LANES : (k + 1) * LANES].astype(jnp.float32)
        local[k, dims:] = jnp.concatenate([labels, spare], axis=0).astype(jnp.bfloat16)

    for copy in len_copies:
        copy.wait_recv()
    all_lens = lens[...].reshape(n_wide, lens.shape[2])
    device = lax.broadcasted_iota(jnp.int32, all_lens.shape, 0)

    def start_of(index):
        return jnp.sum(jnp.where(device < index, all_lens, 0))

    mine = start_of(me)
    rest = lax.rem(n_wide * capacity - mine, LANES)
    across = lax.broadcasted_iota(jnp.int32, (2 * LANES, LANES), 0) - lax.broadcasted_iota(
        jnp.int32, (2 * LANES, LANES), 1
    )
    shift = jnp.where(across == rest, 1.0, 0.0).astype(jnp.bfloat16)

    def placed(half):
        first = lax.rem(half * shard - mine + n_wide * capacity, capacity) // LANES
        loaded = [local[lax.rem(first + k, blocks)] for k in range(shard // LANES + 1)]
        pairs = [jnp.concatenate(loaded[k : k + 2], axis=1) for k in range(shard // LANES)]
        moved = jnp.dot(
            jnp.concatenate(pairs, axis=0), shift, preferred_element_type=jnp.float32
        ).astype(jnp.bfloat16)
        moved = [moved[k * height : (k + 1) * height] for k in range(shard // LANES)]
        each = width // LANES
        return [jnp.concatenate(moved[q * each : (q + 1) * each], axis=1) for q in range(chunks)]

    def bit(j):
        return lax.rem(me // (1 << j), 2)

    wide_copies = {}

    def send_wide(j, q):
        copy = pltpu.make_async_remote_copy(
            src_ref=halves.at[j, 0, q],
            dst_ref=arrived.at[j, q],
            send_sem=wide_send.at[j, q],
            recv_sem=wide_recv.at[j, q],
            device_id=(me + (1 << j) - (2 << j) * bit(j), sub),
            device_id_type=MESH,
        )
        copy.start()
        wide_copies[j, q] = copy

    for q, piece in enumerate(placed(1 - bit(0))):
        halves[0, 0, q] = piece
        send_wide(0, q)
    for q, piece in enumerate(placed(bit(0))):
        halves[0, 1, q] = piece

    edges = []
    for j in range(stages):
        group = me - lax.rem(me, 2 << j)
        edges.append((start_of(group), start_of(group + (1 << j))))

    lane = lax.broadcasted_iota(jnp.int32, (height, width), 1)

    def pick(j, q, position):
        below = jnp.where(position < edges[j][1], 1, 0) + bit(j)
        return jnp.where(below == 1, halves[j, 1, q], arrived[j, q])

    sub_copies = {}

    def advance(j, q):
        wide_copies[j, q].wait_recv()
        if j < stages - 1:
            low = lax.rem(me, 2 << j) * shard + q * width
            first = edges[j][0]

            def position(half):
                offset = half * ((2 << j) * shard) + low - first
                return first + jnp.bitwise_and(offset + lane, (4 << j) * shard - 1)

            halves[j + 1, 0, q] = pick(j, q, position(1 - bit(j + 1)))
            send_wide(j + 1, q)
            halves[j + 1, 1, q] = pick(j, q, position(bit(j + 1)))
            return
        rows = pick(j, q, me * shard + q * width + lane)
        for s in range(n_sub):
            final[q, s, :own_dims] = rows[s * own_dims : (s + 1) * own_dims]
            final[q, s, own_dims:] = rows[dims:]
        for d in range(1, n_sub):
            copy = pltpu.make_async_remote_copy(
                src_ref=final.at[q, sub_peer(d)],
                dst_ref=slices.at[q, sub],
                send_sem=sub_send.at[q, d],
                recv_sem=sub_recv.at[q, d],
                device_id=(me, sub_peer(d)),
                device_id_type=MESH,
            )
            copy.start()
            sub_copies[q, d] = copy

    centroid = lax.broadcasted_iota(jnp.int32, (KCODES, n_sub * width), 0).astype(jnp.float32)
    code_row = lax.broadcasted_iota(jnp.int32, (CODE_ROWS, n_sub * width), 0)

    def refit(q):
        span = slice(q * width, (q + 1) * width)
        pieces = []
        for d in range(n_sub):
            slab = sub_peer(n_sub - d)
            if d:
                sub_copies[q, d].wait_recv()
                piece = slices[q, slab]
            else:
                piece = final[q, slab]
            out_ref[slab, :, span] = piece[:own_dims]
            pieces.append(piece)
        values = jnp.concatenate([piece[:own_dims] for piece in pieces], axis=1)
        labels = jnp.concatenate([piece[own_dims:] for piece in pieces], axis=1).astype(jnp.float32)
        ones = jnp.ones((SUBDIM, n_sub * width), jnp.bfloat16)
        for space in range(own_spaces):
            label = jnp.sum(
                jnp.where(code_row == sub * own_spaces + space, labels, 0.0), axis=0, keepdims=True
            )
            onehot = jnp.where(centroid == label, 1.0, 0.0).astype(jnp.bfloat16)
            left = jnp.concatenate([values[space * SUBDIM : (space + 1) * SUBDIM], ones], axis=0)
            part = lax.dot_general(left, onehot, NT, preferred_element_type=jnp.float32)
            acc[space] = part if q == 0 else acc[space] + part

    for turn in range(chunks + stages):
        for j in reversed(range(stages + 1)):
            q = turn - j
            if 0 <= q < chunks:
                if j < stages:
                    advance(j, q)
                else:
                    refit(q)

    def where_is(t):
        space, rest = divmod(t, 2 * columns)
        row, column = divmod(rest, columns)
        return space, row * 8, slice(column * LANES, (column + 1) * LANES)

    for t in range(n_tiles):
        space, row, span = where_is(t)
        parts[t, :8] = acc[space, row : row + 8, span]
        parts[t, 8:] = acc[space, SUBDIM : SUBDIM + 8, span]

    every = n_tiles == n_wide

    def owner(index):
        return True if every else index < n_tiles

    part_copies = []
    for d in range(1, n_wide):
        peer = wide_peer(d)
        copy = pltpu.make_async_remote_copy(
            src_ref=parts.at[peer if every else lax.rem(peer, n_tiles)],
            dst_ref=parts_in.at[me],
            send_sem=part_send.at[d],
            recv_sem=part_recv.at[d],
            device_id=(peer, sub),
            device_id_type=MESH,
        )
        when(owner(peer))(copy.start)
        part_copies.append((peer, copy))

    tile_copies = []
    for d in range(1, n_wide):
        slot = me if every else lax.rem(me, n_tiles)
        copy = pltpu.make_async_remote_copy(
            src_ref=tile,
            dst_ref=tiles_in.at[slot],
            send_sem=tile_send.at[d],
            recv_sem=tile_recv.at[d],
            device_id=(wide_peer(d), sub),
            device_id_type=MESH,
        )
        tile_copies.append((wide_peer(n_wide - d), copy))

    def add_up():
        slot = me if every else lax.rem(me, n_tiles)
        total = parts[slot]
        for d, (peer, copy) in enumerate(part_copies, 1):
            copy.wait_recv()
            total = total + parts_in[wide_peer(n_wide - d)]
        value = total[:8] / (total[8:] + 1.0)
        tile[...] = value
        for source, copy in tile_copies:
            copy.start()
        tiles_in[slot] = value

    when(owner(me))(add_up)
    for source, copy in tile_copies:
        when(owner(source))(copy.wait_recv)
    for t in range(n_tiles):
        space, row, span = where_is(t)
        book_ref[space, row : row + 8, span] = tiles_in[t]

    for copy in [*len_copies, *wide_copies.values(), *sub_copies.values()]:
        copy.wait_send()
    for peer, copy in part_copies:
        when(owner(peer))(copy.wait_send)

    def drain():
        for source, copy in tile_copies:
            copy.wait_send()

    when(owner(me))(drain)


def solution(mesh):
    n_wide, n_sub = mesh.shape["wide"], mesh.shape["sub"]
    stages = n_wide.bit_length() - 1

    def body(lengths, postings, codes, rotation):
        capacity, dims = postings.shape[1:]
        spaces = codes.shape[1]
        shard = capacity // 2
        width = 256
        chunks = shard // width
        height = dims + CODE_ROWS
        own_dims, own_spaces = dims // n_sub, spaces // n_sub
        n_tiles = own_spaces * (SUBDIM // 8) * (KCODES // LANES)
        bf16, f32 = jnp.bfloat16, jnp.float32
        vmem = pl.BlockSpec(memory_space=pltpu.VMEM)
        dma = pltpu.SemaphoreType.DMA
        return pl.pallas_call(
            functools.partial(kernel, n_wide, n_sub),
            out_shape=(
                jax.ShapeDtypeStruct((n_sub, own_dims, shard), bf16),
                jax.ShapeDtypeStruct((own_spaces, SUBDIM, KCODES), f32),
            ),
            in_specs=[vmem] * 4,
            out_specs=(vmem, vmem),
            scratch_shapes=[
                pltpu.VMEM((n_wide, *lengths.shape), jnp.int32),
                pltpu.VMEM((capacity // LANES, height, LANES), bf16),
                pltpu.VMEM((stages, 2, chunks, height, width), bf16),
                pltpu.VMEM((stages, chunks, height, width), bf16),
                pltpu.VMEM((chunks, n_sub, own_dims + CODE_ROWS, width), bf16),
                pltpu.VMEM((chunks, n_sub, own_dims + CODE_ROWS, width), bf16),
                pltpu.VMEM((own_spaces, 2 * SUBDIM, KCODES), f32),
                pltpu.VMEM((n_tiles, 16, LANES), f32),
                pltpu.VMEM((n_wide, 16, LANES), f32),
                pltpu.VMEM((8, LANES), f32),
                pltpu.VMEM((n_tiles, 8, LANES), f32),
                dma((n_wide,)),
                dma((n_wide,)),
                dma((stages, chunks)),
                dma((stages, chunks)),
                dma((chunks, n_sub)),
                dma((chunks, n_sub)),
                dma((n_wide,)),
                dma((n_wide,)),
                dma((n_wide,)),
                dma((n_wide,)),
            ],
            compiler_params=pltpu.CompilerParams(
                collective_id=0, has_side_effects=True, vmem_limit_bytes=32 * 1024 * 1024
            ),
        )(lengths, postings, codes, rotation)

    return jax.shard_map(
        body,
        mesh=mesh,
        in_specs=(P("sub", "wide"), P("sub", "wide", None), P("sub", None, "wide"), P()),
        out_specs=(P(None, "sub", "wide"), P("sub", None, None)),
        check_vma=False,
    )
```

time: 386 us -> 54.3 us (0.14)
  blocking collectives: 245 us -> 0 us
  local copies, waits for them, and re-layouts: 79.5 us -> 4.61 us
  Pallas kernels: 0 us -> 48.7 us
  other arithmetic: 30 us -> 0 us
  between operations: 14.8 us -> 0.65 us
  starting transfers between devices: 6.71 us -> 0 us
  waiting for transfers between devices: 4.89 us -> 0 us
    all_gather x1 -> x0, blocking collectives: 179 us -> none  [body(): lax.all_gather(code_rows, 'wide', axis=1, tiled=True)]
    pallas_call x0 -> x1, Pallas kernels: none -> 48.7 us  [body(): pl.pallas_call(functools.partial(kernel, n_wide, n_sub), out_shape=(jax.S...]
    gather x16 -> x0, local copies, waits for them, and re-layouts: 48.1 us -> none  [the longest x8 25.6 us: one_shard(): jnp.take(block_rows, safe, axis=0)]
    psum x1 -> x0, blocking collectives: 37.2 us -> none  [body(): full_sums, full_counts = lax.psum((partial_sums, partial_counts), 'wide')]
    unnamed x2 -> x0, blocking collectives: 29.1 us -> none
    dynamic_slice x24 -> x0, local copies, waits for them, and re-layouts: 24.3 us -> none  [the longest x8 10.4 us: one_shard(): lax.dynamic_slice_in_dim(code_piece[0], shard * slots, slots, 0)]
    and x8 -> x0, other arithmetic: 10.3 us -> none  [one_shard(): usable = (within >= 0) & (within < source_total)]
    select_n x24 -> x0, other arithmetic: 7.61 us -> none  [the longest x8 3.82 us: one_shard(): jnp.where(usable[:, None], jnp.take(block_codes, safe, axis=0), code_acc)]
  transfers between devices with their start and end apart: 3 -> 0, of which waited for: 1 -> 0; matrix products, arithmetic and copies ran while one was open for 3% -> 0% of each run, Pallas kernels for 0% -> 0%
where the time goes in v1:
time: 54.3 us; the launch traced here: 54 us
  Pallas kernels  48.7 us (90%)
  local copies, waits for them, and re-layouts  4.61 us (8%)
  between operations  0.65 us (1%)
    pallas_call x1, Pallas kernels, body(): pl.pallas_call(functools.partial(kernel, n_wide, n_sub), out_shape=(jax.S...  48.7 us
    unnamed x10, local copies, waits for them, and re-layouts  4.61 us

profile of v1, /device:TPU:0, one launch (start us, length us, event | category | flops | bytes accessed | tf_op | source)
XLA Modules:
  0.0 54.0 jit_solution(11554831258678438147)
XLA Ops:
  0.6 0.0 copy-start
  0.6 1.0 %copy-done = bf16[1,2048,128]{2,1,0:T(8,128)(2,1)S(1)} copy-done((bf16[1,2048,128]{2,1,0:T(8,128)(2,1)S(1)}, bf16[1,2048,128]{2,1,0:T(8,128)(2,1)}, u32[]{:S(2)}) %copy-start) | copy-done | bytes 524312
  1.7 0.0 copy-start.1
  1.7 0.8 %copy-done.1 = s32[1,8,2048]{2,1,0:T(8,128)S(1)} copy-done((s32[1,8,2048]{2,1,0:T(8,128)S(1)}, s32[1,8,2048]{2,1,0:T(8,128)}, u32[]{:S(2)}) %copy-start.1) | copy-done | bytes 65560
  2.5 0.0 copy-start.2
  2.5 0.8 %copy-done.2 = bf16[128,128]{1,0:T(8,128)(2,1)S(1)} copy-done((bf16[128,128]{1,0:T(8,128)(2,1)S(1)}, bf16[128,128]{1,0:T(8,128)(2,1)}, u32[]{:S(2)}) %copy-start.2) | copy-done | bytes 32792
  3.3 0.0 copy-start.3
  3.3 0.7 %copy-done.3 = s32[1,128]{1,0:T(1,128)S(1)} copy-done((s32[1,128]{1,0:T(1,128)S(1)}, s32[1,128]{1,0:T(1,128)}, u32[]{:S(2)}) %copy-start.3) | copy-done | bytes 536
  3.9 48.7 %shard_map.59 = (bf16[4,32,1024]{2,1,0:T(8,128)(2,1)S(1)}, f32[2,16,256]{2,1,0:T(8,128)S(1)}) custom-call(s32[1,128]{1,0:T(1,128)S(1)} %copy-done.3, bf16[1,2048,128]{2,1,0:T(8,128)(2,1)S(1)} %copy-done, s32[1,8,2048]{2,1,0:T(8,128)S(1)} %copy-done.1, bf16[128,128]{1,0:T(8,128)(2,1)S(1)} %copy-done.2), custom_call_target="tpu_custom_call" | custom-call | tf_op jit(solution)/shard_map/pallas_call | solution.py:325
  52.7 0.7 %copy.8 = bf16[4,32,1024]{2,1,0:T(8,128)(2,1)} copy(bf16[4,32,1024]{2,1,0:T(8,128)(2,1)S(1)} %get-tuple-element.4) | data formatting | bytes 524288
  53.4 0.6 %copy.9 = f32[2,16,256]{2,1,0:T(8,128)} copy(f32[2,16,256]{2,1,0:T(8,128)S(1)} %get-tuple-element.5) | data formatting | bytes 65536
Async XLA Ops:
  0.6 1.0 %copy-start = (bf16[1,2048,128]{2,1,0:T(8,128)(2,1)S(1)}, bf16[1,2048,128]{2,1,0:T(8,128)(2,1)}, u32[]{:S(2)}) copy-start(bf16[1,2048,128]{2,1,0:T(8,128)(2,1)} %post_ref.1) | copy-start | bytes 1572868
  1.7 0.8 %copy-start.1 = (s32[1,8,2048]{2,1,0:T(8,128)S(1)}, s32[1,8,2048]{2,1,0:T(8,128)}, u32[]{:S(2)}) copy-start(s32[1,8,2048]{2,1,0:T(8,128)} %code_ref.1) | copy-start | bytes 196612
  2.5 0.8 %copy-start.2 = (bf16[128,128]{1,0:T(8,128)(2,1)S(1)}, bf16[128,128]{1,0:T(8,128)(2,1)}, u32[]{:S(2)}) copy-start(bf16[128,128]{1,0:T(8,128)(2,1)} %rot_ref.1) | copy-start | bytes 98308
  3.3 0.7 %copy-start.3 = (s32[1,128]{1,0:T(1,128)S(1)}, s32[1,128]{1,0:T(1,128)}, u32[]{:S(2)}) copy-start(s32[1,128]{1,0:T(1,128)} %len_ref.1) | copy-start | bytes 1540

commit v2 on v1

--- a/solution.py
+++ b/solution.py
@@ -10,7 +10,6 @@
 KCODES = 256
 SUBDIM = 16
 LANES = 128
-CODE_ROWS = 16
 MESH = pl.DeviceIdType.MESH
 NT = (((1,), (1,)), ((), ()))
 
@@ -25,17 +24,21 @@
     n_wide,
     n_sub,
     len_ref,
+    post_hbm,
+    code_hbm,
+    rot_hbm,
+    out_ref,
+    book_ref,
     post_ref,
     code_ref,
     rot_ref,
-    out_ref,
-    book_ref,
     lens,
     local,
     halves,
     arrived,
     final,
-    slices,
+    sums,
+    sums_in,
     acc,
     parts,
     parts_in,
@@ -47,10 +50,13 @@
     wide_recv,
     sub_send,
     sub_recv,
+    sum_send,
+    sum_recv,
     part_send,
     part_recv,
     tile_send,
     tile_recv,
+    load,
 ):
     me = lax.axis_index("wide")
     sub = lax.axis_index("sub")
@@ -70,6 +76,14 @@
     def sub_peer(distance):
         return lax.rem(sub + distance, n_sub)
 
+    loads = [
+        pltpu.make_async_copy(source, target, load.at[i])
+        for i, (source, target) in enumerate(
+            ((rot_hbm, rot_ref), (post_hbm, post_ref), (code_hbm, code_ref), (len_ref, lens.at[me]))
+        )
+    ]
+    for copy in loads:
+        copy.start()
     barrier = pltpu.get_barrier_semaphore()
     for d in range(1, n_wide):
         pl.semaphore_signal(barrier, inc=1, device_id=(wide_peer(d), sub), device_id_type=MESH)
@@ -89,22 +103,20 @@
         )
         copy.start()
         len_copies.append(copy)
-    lens[me] = len_ref[...]
-
+
+    loads[0].wait()
     turned = rot_ref[...].astype(jnp.float32).T.astype(jnp.bfloat16)
     blocks = capacity // LANES
     step = capacity // 4
+    loads[1].wait()
     for i in range(4):
         span = slice(i * step, (i + 1) * step)
         block = lax.dot_general(turned, post_ref[0, span, :], NT, preferred_element_type=jnp.float32)
         block = block.astype(jnp.bfloat16)
         for k in range(step // LANES):
-            local[i * (step // LANES) + k, :dims] = block[:, k * LANES : (k + 1) * LANES]
-    spare = jnp.zeros((height - dims - spaces, LANES), jnp.float32)
-    for k in range(blocks):
-        labels = code_ref[0, :, k * LANES : (k + 1) * LANES].astype(jnp.float32)
-        local[k, dims:] = jnp.concatenate([labels, spare], axis=0).astype(jnp.bfloat16)
-
+            local[i * (step // LANES) + k] = block[:, k * LANES : (k + 1) * LANES]
+    loads[2].wait()
+    loads[3].wait()
     for copy in len_copies:
         copy.wait_recv()
     all_lens = lens[...].reshape(n_wide, lens.shape[2])
@@ -183,12 +195,12 @@
             return
         rows = pick(j, q, me * shard + q * width + lane)
         for s in range(n_sub):
-            final[q, s, :own_dims] = rows[s * own_dims : (s + 1) * own_dims]
-            final[q, s, own_dims:] = rows[dims:]
+            final[q, s] = rows[s * own_dims : (s + 1) * own_dims]
+        span = pl.ds(q * width, width)
         for d in range(1, n_sub):
             copy = pltpu.make_async_remote_copy(
                 src_ref=final.at[q, sub_peer(d)],
-                dst_ref=slices.at[q, sub],
+                dst_ref=out_ref.at[sub, :, span],
                 send_sem=sub_send.at[q, d],
                 recv_sem=sub_recv.at[q, d],
                 device_id=(me, sub_peer(d)),
@@ -196,71 +208,80 @@
             )
             copy.start()
             sub_copies[q, d] = copy
-
-    centroid = lax.broadcasted_iota(jnp.int32, (KCODES, n_sub * width), 0).astype(jnp.float32)
-    code_row = lax.broadcasted_iota(jnp.int32, (CODE_ROWS, n_sub * width), 0)
-
-    def refit(q):
-        span = slice(q * width, (q + 1) * width)
-        pieces = []
-        for d in range(n_sub):
-            slab = sub_peer(n_sub - d)
-            if d:
-                sub_copies[q, d].wait_recv()
-                piece = slices[q, slab]
-            else:
-                piece = final[q, slab]
-            out_ref[slab, :, span] = piece[:own_dims]
-            pieces.append(piece)
-        values = jnp.concatenate([piece[:own_dims] for piece in pieces], axis=1)
-        labels = jnp.concatenate([piece[own_dims:] for piece in pieces], axis=1).astype(jnp.float32)
-        ones = jnp.ones((SUBDIM, n_sub * width), jnp.bfloat16)
-        for space in range(own_spaces):
-            label = jnp.sum(
-                jnp.where(code_row == sub * own_spaces + space, labels, 0.0), axis=0, keepdims=True
+        out_ref[sub, :, span] = final[q, sub]
+
+    pieces = 4
+    part_slots = capacity // pieces
+    centroid = lax.broadcasted_iota(jnp.int32, (KCODES, part_slots), 0)
+    slot = lax.broadcasted_iota(jnp.int32, (spaces, capacity), 1)
+    ones = jnp.ones((SUBDIM, part_slots), jnp.bfloat16)
+    code_ref[0] = jnp.where(slot < start_of(me + 1) - mine, code_ref[0], -1)
+
+    def refit(space):
+        total = None
+        for i in range(pieces):
+            span = slice(i * part_slots, (i + 1) * part_slots)
+            labels = code_ref[0, space : space + 1, span]
+            onehot = jnp.where(centroid == labels, 1.0, 0.0).astype(jnp.bfloat16)
+            each = part_slots // LANES
+            values = [
+                local[i * each + k, space * SUBDIM : (space + 1) * SUBDIM] for k in range(each)
+            ]
+            left = jnp.concatenate([jnp.concatenate(values, axis=1), ones], axis=0)
+            part = lax.dot_general(left, onehot, NT, preferred_element_type=jnp.float32)
+            total = part if total is None else total + part
+        sums[space // own_spaces, space % own_spaces] = total[: SUBDIM + 8]
+
+    sum_copies = []
+
+    def send_sums():
+        for d in range(1, n_sub):
+            copy = pltpu.make_async_remote_copy(
+                src_ref=sums.at[sub_peer(d)],
+                dst_ref=sums_in.at[sub],
+                send_sem=sum_send.at[d],
+                recv_sem=sum_recv.at[d],
+                device_id=(me, sub_peer(d)),
+                device_id_type=MESH,
             )
-            onehot = jnp.where(centroid == label, 1.0, 0.0).astype(jnp.bfloat16)
-            left = jnp.concatenate([values[space * SUBDIM : (space + 1) * SUBDIM], ones], axis=0)
-            part = lax.dot_general(left, onehot, NT, preferred_element_type=jnp.float32)
-            acc[space] = part if q == 0 else acc[space] + part
-
-    for turn in range(chunks + stages):
-        for j in reversed(range(stages + 1)):
-            q = turn - j
-            if 0 <= q < chunks:
-                if j < stages:
-                    advance(j, q)
-                else:
-                    refit(q)
+            copy.start()
+            sum_copies.append(copy)
 
     def where_is(t):
         space, rest = divmod(t, 2 * columns)
         row, column = divmod(rest, columns)
         return space, row * 8, slice(column * LANES, (column + 1) * LANES)
 
-    for t in range(n_tiles):
-        space, row, span = where_is(t)
-        parts[t, :8] = acc[space, row : row + 8, span]
-        parts[t, 8:] = acc[space, SUBDIM : SUBDIM + 8, span]
-
     every = n_tiles == n_wide
 
     def owner(index):
         return True if every else index < n_tiles
 
     part_copies = []
-    for d in range(1, n_wide):
-        peer = wide_peer(d)
-        copy = pltpu.make_async_remote_copy(
-            src_ref=parts.at[peer if every else lax.rem(peer, n_tiles)],
-            dst_ref=parts_in.at[me],
-            send_sem=part_send.at[d],
-            recv_sem=part_recv.at[d],
-            device_id=(peer, sub),
-            device_id_type=MESH,
-        )
-        when(owner(peer))(copy.start)
-        part_copies.append((peer, copy))
+
+    def send_parts():
+        for d, copy in enumerate(sum_copies, 1):
+            copy.wait_recv()
+        total = sums[sub]
+        for d in range(1, n_sub):
+            total = total + sums_in[sub_peer(n_sub - d)]
+        acc[...] = total
+        for t in range(n_tiles):
+            space, row, span = where_is(t)
+            parts[t, :8] = acc[space, row : row + 8, span]
+            parts[t, 8:] = acc[space, SUBDIM : SUBDIM + 8, span]
+        for d in range(1, n_wide):
+            peer = wide_peer(d)
+            copy = pltpu.make_async_remote_copy(
+                src_ref=parts.at[peer if every else lax.rem(peer, n_tiles)],
+                dst_ref=parts_in.at[me],
+                send_sem=part_send.at[d],
+                recv_sem=part_recv.at[d],
+                device_id=(peer, sub),
+                device_id_type=MESH,
+            )
+            when(owner(peer))(copy.start)
+            part_copies.append((peer, copy))
 
     tile_copies = []
     for d in range(1, n_wide):
@@ -287,14 +308,42 @@
             copy.start()
         tiles_in[slot] = value
 
-    when(owner(me))(add_up)
-    for source, copy in tile_copies:
-        when(owner(source))(copy.wait_recv)
-    for t in range(n_tiles):
-        space, row, span = where_is(t)
-        book_ref[space, row : row + 8, span] = tiles_in[t]
-
-    for copy in [*len_copies, *wide_copies.values(), *sub_copies.values()]:
+    def send_tile():
+        when(owner(me))(add_up)
+
+    def finish():
+        for source, copy in tile_copies:
+            when(owner(source))(copy.wait_recv)
+        for t in range(n_tiles):
+            space, row, span = where_is(t)
+            book_ref[space, row : row + 8, span] = tiles_in[t]
+
+    def refits(first, last):
+        def run():
+            for space in range(first, last):
+                refit(space)
+
+        return run
+
+    beside = [refits(i * spaces // 4, (i + 1) * spaces // 4) for i in range(4)]
+    beside += [send_sums, None, send_parts, None, send_tile]
+    for turn in range(chunks + stages - 1):
+        for j in range(stages):
+            q = turn - j
+            if 0 <= q < chunks:
+                if beside:
+                    task = beside.pop(0)
+                    if task is not None:
+                        task()
+                advance(j, q)
+    for task in beside:
+        if task is not None:
+            task()
+    finish()
+    for copy in sub_copies.values():
+        copy.wait_recv()
+
+    for copy in [*len_copies, *wide_copies.values(), *sub_copies.values(), *sum_copies]:
         copy.wait_send()
     for peer, copy in part_copies:
         when(owner(peer))(copy.wait_send)
@@ -316,7 +365,7 @@
         shard = capacity // 2
         width = 256
         chunks = shard // width
-        height = dims + CODE_ROWS
+        height = dims
         own_dims, own_spaces = dims // n_sub, spaces // n_sub
         n_tiles = own_spaces * (SUBDIM // 8) * (KCODES // LANES)
         bf16, f32 = jnp.bfloat16, jnp.float32
@@ -328,16 +377,20 @@
                 jax.ShapeDtypeStruct((n_sub, own_dims, shard), bf16),
                 jax.ShapeDtypeStruct((own_spaces, SUBDIM, KCODES), f32),
             ),
-            in_specs=[vmem] * 4,
+            in_specs=[pl.BlockSpec(memory_space=pltpu.HBM)] * 4,
             out_specs=(vmem, vmem),
             scratch_shapes=[
+                pltpu.VMEM(postings.shape, bf16),
+                pltpu.VMEM(codes.shape, jnp.int32),
+                pltpu.VMEM(rotation.shape, bf16),
                 pltpu.VMEM((n_wide, *lengths.shape), jnp.int32),
                 pltpu.VMEM((capacity // LANES, height, LANES), bf16),
                 pltpu.VMEM((stages, 2, chunks, height, width), bf16),
                 pltpu.VMEM((stages, chunks, height, width), bf16),
-                pltpu.VMEM((chunks, n_sub, own_dims + CODE_ROWS, width), bf16),
-                pltpu.VMEM((chunks, n_sub, own_dims + CODE_ROWS, width), bf16),
-                pltpu.VMEM((own_spaces, 2 * SUBDIM, KCODES), f32),
+                pltpu.VMEM((chunks, n_sub, own_dims, width), bf16),
+                pltpu.VMEM((n_sub, own_spaces, SUBDIM + 8, KCODES), f32),
+                pltpu.VMEM((n_sub, own_spaces, SUBDIM + 8, KCODES), f32),
+                pltpu.VMEM((own_spaces, SUBDIM + 8, KCODES), f32),
                 pltpu.VMEM((n_tiles, 16, LANES), f32),
                 pltpu.VMEM((n_wide, 16, LANES), f32),
                 pltpu.VMEM((8, LANES), f32),
@@ -348,13 +401,16 @@
                 dma((stages, chunks)),
                 dma((chunks, n_sub)),
                 dma((chunks, n_sub)),
-                dma((n_wide,)),
-                dma((n_wide,)),
-                dma((n_wide,)),
-                dma((n_wide,)),
+                dma((n_sub,)),
+                dma((n_sub,)),
+                dma((n_wide,)),
+                dma((n_wide,)),
+                dma((n_wide,)),
+                dma((n_wide,)),
+                dma((4,)),
             ],
             compiler_params=pltpu.CompilerParams(
-                collective_id=0, has_side_effects=True, vmem_limit_bytes=32 * 1024 * 1024
+                collective_id=0, has_side_effects=True, vmem_limit_bytes=60 * 1024 * 1024
             ),
         )(lengths, postings, codes, rotation)
 

time: 54.3 us -> 41.1 us (0.76)
  Pallas kernels: 48.7 us -> 38 us
  local copies, waits for them, and re-layouts: 4.61 us -> 2.29 us
    pallas_call x1, Pallas kernels: 48.7 us -> 38 us  [body(): pl.pallas_call(functools.partial(kernel, n_wide, n_sub), out_shape=(jax.S...]
    unnamed x10 -> x4, local copies, waits for them, and re-layouts: 4.61 us -> 2.29 us
where the time goes in v2:
time: 41.1 us; the launch traced here: 40.9 us
  Pallas kernels  38 us (92%)
  local copies, waits for them, and re-layouts  2.29 us (6%)
  between operations  0.65 us (2%)
    pallas_call x1, Pallas kernels, body(): pl.pallas_call(functools.partial(kernel, n_wide, n_sub), out_shape=(jax.S...  38 us
    unnamed x4, local copies, waits for them, and re-layouts  2.29 us

profile of v2, /device:TPU:0, one launch (start us, length us, event | category | flops | bytes accessed | tf_op | source)
XLA Modules:
  0.0 40.9 jit_solution(3331450374251283225)
XLA Ops:
  0.6 38.0 %shard_map.59 = (bf16[4,32,1024]{2,1,0:T(8,128)(2,1)}, f32[2,16,256]{2,1,0:T(8,128)}) custom-call(s32[1,128]{1,0:T(1,128)} %len_ref.1, bf16[1,2048,128]{2,1,0:T(8,128)(2,1)} %post_hbm.1, s32[1,8,2048]{2,1,0:T(8,128)} %code_hbm.1, bf16[128,128]{1,0:T(8,128)(2,1)} %rot_hbm.1), custom_call_target="tpu_custom_call" | custom-call | tf_op jit(solution)/shard_map/pallas_call | solution.py:374
  38.6 0.0 copy-start
  38.6 1.7 %copy.8 = bf16[4,32,1024]{2,1,0:T(8,128)(2,1)} copy(bf16[4,32,1024]{2,1,0:T(8,128)(2,1)} %get-tuple-element.4) | data formatting | bytes 524288
  40.3 0.0 copy-done
  40.3 0.6 %copy.9 = f32[2,16,256]{2,1,0:T(8,128)} copy(f32[2,16,256]{2,1,0:T(8,128)S(1)} %copy-done) | data formatting | bytes 65536
Async XLA Ops:
  38.6 1.7 %copy-start = (f32[2,16,256]{2,1,0:T(8,128)S(1)}, f32[2,16,256]{2,1,0:T(8,128)}, u32[]{:S(2)}) copy-start(f32[2,16,256]{2,1,0:T(8,128)} %get-tuple-element.5) | copy-start | bytes 98308

commit v3 on v2

--- a/solution.py
+++ b/solution.py
@@ -327,15 +327,12 @@
 
     beside = [refits(i * spaces // 4, (i + 1) * spaces // 4) for i in range(4)]
     beside += [send_sums, None, send_parts, None, send_tile]
-    for turn in range(chunks + stages - 1):
-        for j in range(stages):
-            q = turn - j
-            if 0 <= q < chunks:
-                if beside:
-                    task = beside.pop(0)
-                    if task is not None:
-                        task()
-                advance(j, q)
+    for j, q in ((j, q) for j in range(stages) for q in range(chunks)):
+        if beside:
+            task = beside.pop(0)
+            if task is not None:
+                task()
+        advance(j, q)
     for task in beside:
         if task is not None:
             task()

time: 41.1 us -> 39.8 us (0.968)
  Pallas kernels: 38 us -> 36.8 us
    pallas_call x1, Pallas kernels: 38 us -> 36.8 us  [body(): pl.pallas_call(functools.partial(kernel, n_wide, n_sub), out_shape=(jax.S...]
where the time goes in v3:
time: 39.8 us; the launch traced here: 39.7 us
  Pallas kernels  36.8 us (92%)
  local copies, waits for them, and re-layouts  2.29 us (6%)
  between operations  0.65 us (2%)
    pallas_call x1, Pallas kernels, body(): pl.pallas_call(functools.partial(kernel, n_wide, n_sub), out_shape=(jax.S...  36.8 us
    unnamed x4, local copies, waits for them, and re-layouts  2.29 us

profile of v3, /device:TPU:0, one launch (start us, length us, event | category | flops | bytes accessed | tf_op | source)
XLA Modules:
  0.0 39.7 jit_solution(12990257424947014475)
XLA Ops:
  0.6 36.8 %shard_map.59 = (bf16[4,32,1024]{2,1,0:T(8,128)(2,1)}, f32[2,16,256]{2,1,0:T(8,128)}) custom-call(s32[1,128]{1,0:T(1,128)} %len_ref.1, bf16[1,2048,128]{2,1,0:T(8,128)(2,1)} %post_hbm.1, s32[1,8,2048]{2,1,0:T(8,128)} %code_hbm.1, bf16[128,128]{1,0:T(8,128)(2,1)} %rot_hbm.1), custom_call_target="tpu_custom_call" | custom-call | tf_op jit(solution)/shard_map/pallas_call | solution.py:371
  37.4 0.0 copy-start
  37.4 1.7 %copy.8 = bf16[4,32,1024]{2,1,0:T(8,128)(2,1)} copy(bf16[4,32,1024]{2,1,0:T(8,128)(2,1)} %get-tuple-element.4) | data formatting | bytes 524288
  39.1 0.0 copy-done
  39.1 0.6 %copy.9 = f32[2,16,256]{2,1,0:T(8,128)} copy(f32[2,16,256]{2,1,0:T(8,128)S(1)} %copy-done) | data formatting | bytes 65536
Async XLA Ops:
  37.4 1.7 %copy-start = (f32[2,16,256]{2,1,0:T(8,128)S(1)}, f32[2,16,256]{2,1,0:T(8,128)}, u32[]{:S(2)}) copy-start(f32[2,16,256]{2,1,0:T(8,128)} %get-tuple-element.5) | copy-start | bytes 98308

commit v4 on v3

--- a/solution.py
+++ b/solution.py
@@ -117,6 +117,47 @@
             local[i * (step // LANES) + k] = block[:, k * LANES : (k + 1) * LANES]
     loads[2].wait()
     loads[3].wait()
+    pieces = 4
+    part_slots = capacity // pieces
+    centroid = lax.broadcasted_iota(jnp.int32, (KCODES, part_slots), 0)
+    slot = lax.broadcasted_iota(jnp.int32, (spaces, capacity), 1)
+    ones = jnp.ones((SUBDIM, part_slots), jnp.bfloat16)
+    code_ref[0] = jnp.where(slot < jnp.sum(lens[me]), code_ref[0], -1)
+
+    def refit(space):
+        total = None
+        for i in range(pieces):
+            span = slice(i * part_slots, (i + 1) * part_slots)
+            labels = code_ref[0, space : space + 1, span]
+            onehot = jnp.where(centroid == labels, 1.0, 0.0).astype(jnp.bfloat16)
+            each = part_slots // LANES
+            values = [
+                local[i * each + k, space * SUBDIM : (space + 1) * SUBDIM] for k in range(each)
+            ]
+            left = jnp.concatenate([jnp.concatenate(values, axis=1), ones], axis=0)
+            part = lax.dot_general(left, onehot, NT, preferred_element_type=jnp.float32)
+            total = part if total is None else total + part
+        sums[space // own_spaces, space % own_spaces] = total[: SUBDIM + 8]
+
+    sum_copies = []
+
+    def send_sums():
+        for d in range(1, n_sub):
+            copy = pltpu.make_async_remote_copy(
+                src_ref=sums.at[sub_peer(d)],
+                dst_ref=sums_in.at[sub],
+                send_sem=sum_send.at[d],
+                recv_sem=sum_recv.at[d],
+                device_id=(me, sub_peer(d)),
+                device_id_type=MESH,
+            )
+            copy.start()
+            sum_copies.append(copy)
+
+    for space in range(spaces):
+        refit(space)
+    send_sums()
+
     for copy in len_copies:
         copy.wait_recv()
     all_lens = lens[...].reshape(n_wide, lens.shape[2])
@@ -209,43 +250,6 @@
             copy.start()
             sub_copies[q, d] = copy
         out_ref[sub, :, span] = final[q, sub]
-
-    pieces = 4
-    part_slots = capacity // pieces
-    centroid = lax.broadcasted_iota(jnp.int32, (KCODES, part_slots), 0)
-    slot = lax.broadcasted_iota(jnp.int32, (spaces, capacity), 1)
-    ones = jnp.ones((SUBDIM, part_slots), jnp.bfloat16)
-    code_ref[0] = jnp.where(slot < start_of(me + 1) - mine, code_ref[0], -1)
-
-    def refit(space):
-        total = None
-        for i in range(pieces):
-            span = slice(i * part_slots, (i + 1) * part_slots)
-            labels = code_ref[0, space : space + 1, span]
-            onehot = jnp.where(centroid == labels, 1.0, 0.0).astype(jnp.bfloat16)
-            each = part_slots // LANES
-            values = [
-                local[i * each + k, space * SUBDIM : (space + 1) * SUBDIM] for k in range(each)
-            ]
-            left = jnp.concatenate([jnp.concatenate(values, axis=1), ones], axis=0)
-            part = lax.dot_general(left, onehot, NT, preferred_element_type=jnp.float32)
-            total = part if total is None else total + part
-        sums[space // own_spaces, space % own_spaces] = total[: SUBDIM + 8]
-
-    sum_copies = []
-
-    def send_sums():
-        for d in range(1, n_sub):
-            copy = pltpu.make_async_remote_copy(
-                src_ref=sums.at[sub_peer(d)],
-                dst_ref=sums_in.at[sub],
-                send_sem=sum_send.at[d],
-                recv_sem=sum_recv.at[d],
-                device_id=(me, sub_peer(d)),
-                device_id_type=MESH,
-            )
-            copy.start()
-            sum_copies.append(copy)
 
     def where_is(t):
         space, rest = divmod(t, 2 * columns)
@@ -318,15 +322,7 @@
             space, row, span = where_is(t)
             book_ref[space, row : row + 8, span] = tiles_in[t]
 
-    def refits(first, last):
-        def run():
-            for space in range(first, last):
-                refit(space)
-
-        return run
-
-    beside = [refits(i * spaces // 4, (i + 1) * spaces // 4) for i in range(4)]
-    beside += [send_sums, None, send_parts, None, send_tile]
+    beside = [None, None, None, None, send_parts, None, None, send_tile]
     for j, q in ((j, q) for j in range(stages) for q in range(chunks)):
         if beside:
             task = beside.pop(0)

time: 39.8 us -> 38.9 us (0.977)
  Pallas kernels: 36.8 us -> 35.8 us
    pallas_call x1, Pallas kernels: 36.8 us -> 35.8 us  [body(): pl.pallas_call(functools.partial(kernel, n_wide, n_sub), out_shape=(jax.S...]
where the time goes in v4:
time: 38.9 us; the launch traced here: 38.7 us
  Pallas kernels  35.8 us (92%)
  local copies, waits for them, and re-layouts  2.29 us (6%)
  between operations  0.65 us (2%)
    pallas_call x1, Pallas kernels, body(): pl.pallas_call(functools.partial(kernel, n_wide, n_sub), out_shape=(jax.S...  35.8 us
    unnamed x4, local copies, waits for them, and re-layouts  2.29 us

profile of v4, /device:TPU:0, one launch (start us, length us, event | category | flops | bytes accessed | tf_op | source)
XLA Modules:
  0.0 38.7 jit_solution(11116346670882170775)
XLA Ops:
  0.6 35.8 %shard_map.59 = (bf16[4,32,1024]{2,1,0:T(8,128)(2,1)}, f32[2,16,256]{2,1,0:T(8,128)}) custom-call(s32[1,128]{1,0:T(1,128)} %len_ref.1, bf16[1,2048,128]{2,1,0:T(8,128)(2,1)} %post_hbm.1, s32[1,8,2048]{2,1,0:T(8,128)} %code_hbm.1, bf16[128,128]{1,0:T(8,128)(2,1)} %rot_hbm.1), custom_call_target="tpu_custom_call" | custom-call | tf_op jit(solution)/shard_map/pallas_call | solution.py:367
  36.4 0.0 copy-start
  36.4 1.7 %copy.8 = bf16[4,32,1024]{2,1,0:T(8,128)(2,1)} copy(bf16[4,32,1024]{2,1,0:T(8,128)(2,1)} %get-tuple-element.4) | data formatting | bytes 524288
  38.1 0.0 copy-done
  38.1 0.6 %copy.9 = f32[2,16,256]{2,1,0:T(8,128)} copy(f32[2,16,256]{2,1,0:T(8,128)S(1)} %copy-done) | data formatting | bytes 65536
Async XLA Ops:
  36.4 1.7 %copy-start = (f32[2,16,256]{2,1,0:T(8,128)S(1)}, f32[2,16,256]{2,1,0:T(8,128)}, u32[]{:S(2)}) copy-start(f32[2,16,256]{2,1,0:T(8,128)} %get-tuple-element.5) | copy-start | bytes 98308
